TPU v7x, 512 devices: a whole 4x8x8 slice. The times are simulated.
512 devices in a mesh: row: 32 (over z, y_lo), col: 16 (over x, y_hi, core).
Axes of the slice: x: 4, y: 8 (y_hi: 2, y_lo: 4; y = y_hi * 4 + y_lo), z: 8, core: 2. Of those that a mesh axis runs over, the one named last changes fastest.
Arguments:
- features: bfloat16 [131072, 128], P(('col', 'row')), may hold values from -6 to 6
- weight: bfloat16 [128, 256], replicated, may hold values from -0.5 to 0.5
- bias: float32 [256], replicated, may hold values from -3 to 3
- grad_out: bfloat16 [131072, 256], P(('row', 'col')), may hold values from -6 to 6
- tile_values: bfloat16 [32, 16, 128, 128, 128], P('row', 'col'), may hold values from -0.1875 to 0.1875
- tile_rows: int32 [32, 16, 128], P('row', 'col'), may hold values from 0 to 31
- tile_cols: int32 [32, 16, 128], P('row', 'col'), may hold values from 0 to 63
- tile_count: int32 [32, 16], P('row', 'col'), may hold values from 42 to 128, as said below
Outputs:
- hidden: bfloat16 [131072, 256], P(('row', 'col'))
- grad_weight: float32 [128, 256], replicated
- grad_bias: float32 [256], replicated
- grad_features: bfloat16 [131072, 128], P(('col', 'row'))
Inputs may be any that keep to these rules, and one draw needn't show every extreme that they name: `tile_count`: slots below the count are live; some block has all 128 slots live.
All inputs are finite; a program needn't handle non-finite values.
Results may differ from a plain program's by a relative error of at most 0.03.
Values may be sent and summed in bfloat16 or wider, within the bound.
A program may use at most 64 MiB of HBM per device.

v0:
```python
import jax
import jax.numpy as jnp
from jax import lax
from jax.sharding import PartitionSpec as P


def per_device(features, weight, bias, grad_out, tile_values, tile_rows, tile_cols, tile_count):
    values = tile_values[0, 0]
    slot_rows = tile_rows[0, 0]
    slot_cols = tile_cols[0, 0]
    tile_size = values.shape[1]
    width_in = features.shape[1]
    node_rows = features.shape[0]
    live = (jnp.arange(values.shape[0]) < tile_count[0, 0]).astype(values.dtype)
    values = values * live[:, None, None]
    panel = lax.all_gather(features, "row", axis=0, tiled=True)
    panel_tiles = panel.reshape(-1, tile_size, width_in)
    picked = panel_tiles[slot_cols]
    products = jnp.einsum("kij,kjf->kif", values, picked, preferred_element_type=jnp.float32)
    row_segments = lax.axis_size("col") * node_rows // tile_size
    partial_value = jax.ops.segment_sum(products, slot_rows, num_segments=row_segments).reshape(
        -1, width_in
    )
    aggregate = lax.psum_scatter(
        partial_value.astype(jnp.bfloat16), "col", scatter_dimension=0, tiled=True
    )
    preact = jnp.dot(aggregate, weight, preferred_element_type=jnp.float32) + bias
    sigmoid_pre = jax.nn.sigmoid(preact)
    hidden = (preact * sigmoid_pre).astype(jnp.bfloat16)
    slope_factor = sigmoid_pre * (1.0 + preact * (1.0 - sigmoid_pre))
    grad_pre = (grad_out.astype(jnp.float32) * slope_factor).astype(jnp.bfloat16)
    local_weight = jnp.dot(aggregate.T, grad_pre, preferred_element_type=jnp.float32)
    local_bias = jnp.sum(grad_pre.astype(jnp.float32), axis=0)
    grad_weight, grad_bias = lax.psum((local_weight, local_bias), ("row", "col"))
    grad_block = lax.all_gather(grad_pre, "col", axis=0, tiled=True)
    block_aggregate = jnp.dot(grad_block, weight.T, preferred_element_type=jnp.float32).astype(
        jnp.bfloat16
    )
    block_tiles = block_aggregate.reshape(-1, tile_size, width_in)
    picked_back = block_tiles[slot_rows]
    back_products = jnp.einsum(
        "kji,kjf->kif", values, picked_back, preferred_element_type=jnp.float32
    )
    col_segments = lax.axis_size("row") * node_rows // tile_size
    partial_back = jax.ops.segment_sum(back_products, slot_cols, num_segments=col_segments).reshape(
        -1, width_in
    )
    grad_features = lax.psum_scatter(
        partial_back.astype(jnp.bfloat16), "row", scatter_dimension=0, tiled=True
    )
    return (hidden, grad_weight, grad_bias, grad_features)


def solution(mesh):
    return jax.shard_map(
        per_device,
        mesh=mesh,
        in_specs=(
            P(("col", "row"), None),
            P(),
            P(),
            P(("row", "col"), None),
            P("row", "col", None, None, None),
            P("row", "col", None),
            P("row", "col", None),
            P("row", "col"),
        ),
        out_specs=(P(("row", "col"), None), P(), P(), P(("col", "row"), None)),
        check_vma=False,
    )
```

profile of v0, /device:TPU:6, one launch (start us, length us, event | category | flops | bytes accessed | tf_op | source)
XLA Modules:
  0.0 795.0 jit_solution(7992885801044690359)
XLA Ops:
  7.2 0.0 copy-start
  7.2 0.0 all-gather.3.cloned.1.call-start
  7.2 0.7 all-gather.3.cloned.1.call-update
  7.9 0.0 reduce-scatter.3.cloned.1.call-start
  8.6 0.7 fusion.4
  9.3 163.6 %all-gather.3.cloned.1.call-done = bf16[8192,128]{1,0:T(8,128)(2,1)} async-done(((bf16[256,128]{1,0:T(8,128)(2,1)}), bf16[8192,128]{1,0:T(8,128)(2,1)}) %all-gather.3.cloned.1.call-update) | async-done | bytes 2097168 | tf_op jit(solution)/shard_map/all_gather | solution.py:16
  172.9 4.6 gather_fusion
  177.5 8.0 %fusion.1 = f32[128,128,128]{2,1,0:T(8,128)} fusion(bf16[128,128,128]{2,1,0:T(8,128)(2,1)} %gather_fusion, bf16[1,1,128,128,128]{4,3,2,1,0:T(8,128)(2,1)} %param.12, bf16[128]{0:T(256)(128)(2,1)S(1)} %compare_convert_fusion), kind=kOutput, calls=%fused_computation.7 | convolution fusion | flops 538968064 | bytes 16777472 | tf_op jit(solution)/shard_map/kij,kjf->kif/dot_general | solution.py:19
  185.5 0.2 broadcast_in_dim.4
  185.8 17.1 %scatter_fusion = f32[32,128,128]{2,1,0:T(8,128)S(1)} fusion(f32[32,128,128]{2,1,0:T(8,128)S(1)} %broadcast_in_dim.4, s32[128]{0:T(128)S(1)} %bitcast.32, f32[128,128,128]{2,1,0:T(8,128)} %fusion.1), kind=kCustom, calls=%fused_computation.2 | custom fusion | flops 2097152 | bytes 25166336 | tf_op jit(solution)/shard_map/scatter-add | solution.py:21
  202.9 1.1 convert_element_type.35
  204.0 0.0 reduce-scatter.3.cloned.1.call-update
  204.0 0.0 all-gather.5.cloned.1.call-start
  204.1 86.8 %reduce-scatter.3.cloned.1.call-done = bf16[256,128]{1,0:T(8,128)(2,1)} async-done(((bf16[4096,128]{1,0:T(8,128)(2,1)}), bf16[256,128]{1,0:T(8,128)(2,1)}) %reduce-scatter.3.cloned.1.call-update) | async-done | bytes 65552 | tf_op jit(solution)/shard_map/reduce_scatter | solution.py:24
  290.9 1.8 convert_reduce_fusion
  292.7 0.0 all-gather.5.cloned.1.call-update
  292.8 0.0 all-reduce.2.cloned.1.call-start
  292.8 1.8 fusion.6
  294.6 0.0 all-reduce.2.cloned.1.call-update
  294.6 0.0 reduce-scatter.5.cloned.1.call-start
  294.7 61.8 %all-gather.5.cloned.1.call-done = bf16[4096,256]{1,0:T(8,128)(2,1)} async-done(((bf16[256,256]{1,0:T(8,128)(2,1)}), bf16[4096,256]{1,0:T(8,128)(2,1)}) %all-gather.5.cloned.1.call-update) | async-done | bytes 2097168 | tf_op jit(solution)/shard_map/all_gather | solution.py:35
  356.5 2.3 convolution_convert_fusion
  358.8 3.1 gather_fusion.1
  361.9 8.4 %fusion = f32[128,128,128]{2,1,0:T(8,128)} fusion(bf16[128,128,128]{2,1,0:T(8,128)(2,1)} %gather_fusion.1, bf16[1,1,128,128,128]{4,3,2,1,0:T(8,128)(2,1)} %param.12, bf16[128]{0:T(256)(128)(2,1)S(1)} %compare_convert_fusion), kind=kOutput, calls=%fused_computation.6 | convolution fusion | flops 538968064 | bytes 16777472 | tf_op jit(solution)/shard_map/kji,kjf->kif/dot_general | solution.py:41
  370.3 2.5 broadcast_in_dim.5
  372.7 26.7 %scatter_fusion.1 = f32[64,128,128]{2,1,0:T(8,128)} fusion(f32[64,128,128]{2,1,0:T(8,128)} %broadcast_in_dim.5, s32[128]{0:T(128)S(1)} %bitcast.33, f32[128,128,128]{2,1,0:T(8,128)} %fusion), kind=kCustom, calls=%fused_computation.3 | custom fusion | flops 2097152 | bytes 25166336 | tf_op jit(solution)/shard_map/scatter-add | solution.py:45
  399.4 3.9 convert_element_type.42
  403.3 0.0 reduce-scatter.5.cloned.1.call-update
  403.3 100.3 %psum.15 = f32[256]{0:T(256)} all-reduce(f32[256]{0:T(256)S(1)} %get-tuple-element.4), channel_id=1, replica_groups=mesh['row'=32,'col'=16] {'row','col'}, use_global_device_ids=true, to_apply=%region_4.0 | all-reduce | flops 256 | bytes 2048 | tf_op jit(solution)/shard_map/psum | solution.py:34
  503.7 117.1 %all-reduce.2.cloned.1.call-done = f32[128,256]{1,0:T(8,128)} async-done(((f32[128,256]{1,0:T(8,128)}), f32[128,256]{1,0:T(8,128)}) %all-reduce.2.cloned.1.call-update) | async-done | bytes 131088 | tf_op jit(solution)/shard_map/psum | solution.py:34
  620.8 166.1 %reduce-scatter.5.cloned.1.call-done = bf16[256,128]{1,0:T(8,128)(2,1)} async-done(((bf16[8192,128]{1,0:T(8,128)(2,1)}), bf16[256,128]{1,0:T(8,128)(2,1)}) %reduce-scatter.5.cloned.1.call-update) | async-done | bytes 65552 | tf_op jit(solution)/shard_map/reduce_scatter | solution.py:48
  786.9 1.6 copy.18
  (13 shorter events, 0.0 us)
Async XLA Ops:
  7.2 283.7 %copy-start = (bf16[128,256]{1,0:T(8,128)(2,1)S(1)}, bf16[128,256]{1,0:T(8,128)(2,1)}, u32[]{:S(2)}) copy-start(bf16[128,256]{1,0:T(8,128)(2,1)} %param.9) | copy-start | bytes 196612
  7.2 165.7 %all-gather.3.cloned.1.call-start = ((), (), s32[]{:S(2)}) async-start(), calls=%async_computation.2 | async-start | bytes 2162688 | tf_op jit(solution)/shard_map/all_gather | solution.py:16
  7.9 283.0 %reduce-scatter.3.cloned.1.call-start = ((), (), s32[]{:S(2)}) async-start(), calls=%async_computation.3 | async-start | bytes 1114112 | tf_op jit(solution)/shard_map/reduce_scatter | solution.py:24
  177.5 8.2 %copy-start.1 = (s32[1,1,128]{2,1,0:T(1,128)S(1)}, s32[1,1,128]{2,1,0:T(1,128)}, u32[]{:S(2)}) copy-start(s32[1,1,128]{2,1,0:T(1,128)} %param.13) | copy-start | bytes 1540
  202.8 88.1 %copy-start.3 = (bf16[256,256]{1,0:T(8,128)(2,1)S(1)}, bf16[256,256]{1,0:T(8,128)(2,1)}, u32[]{:S(2)}) copy-start(bf16[256,256]{1,0:T(8,128)(2,1)} %param.11) | copy-start | bytes 393220
  202.8 88.1 %copy-start.4 = (f32[256]{0:T(256)S(1)}, f32[256]{0:T(256)}, u32[]{:S(2)}) copy-start(f32[256]{0:T(256)} %param.10) | copy-start | bytes 3076
  204.0 152.5 %all-gather.5.cloned.1.call-start = ((), (), s32[]{:S(2)}) async-start(), calls=%async_computation.5 | async-start | bytes 2228224 | tf_op jit(solution)/shard_map/all_gather | solution.py:35
  292.8 328.0 %all-reduce.2.cloned.1.call-start = ((), (), s32[]{:S(2)}) async-start(), calls=%async_computation.4 | async-start | bytes 262144 | tf_op jit(solution)/shard_map/psum | solution.py:34
  294.6 492.2 %reduce-scatter.5.cloned.1.call-start = ((), (), s32[]{:S(2)}) async-start(), calls=%async_computation.6 | async-start | bytes 2162688 | tf_op jit(solution)/shard_map/reduce_scatter | solution.py:48
  370.3 2.5 copy-start.2
Sparse Core Ops, SparseCore 0:
  10.1 162.7 all-gather.2
  204.1 86.7 reduce-scatter.2
  295.3 61.2 all-gather.4
  362.2 258.5 all-reduce.1
  624.0 162.7 reduce-scatter.4
where the time goes:
time: 796 us; the launch traced here: 795 us
  waiting for transfers between devices  596 us (75%)
  blocking collectives  100 us (13%)
  other arithmetic  49.5 us (6%)
  matrix products  22.3 us (3%)
  between operations  14.5 us (2%)
  local copies, waits for them, and re-layouts  12 us (2%)
    reduce_scatter x1, waiting for transfers between devices, per_device(): lax.psum_scatter(partial_back.astype(jnp.bfloat16), 'row', scatter_dimens...  166 us
    all_gather x1, waiting for transfers between devices, per_device(): panel = lax.all_gather(features, 'row', axis=0, tiled=True)  164 us
    psum x1, waiting for transfers between devices, per_device(): lax.psum((local_weight, local_bias), ('row', 'col'))  117 us
    psum x1, blocking collectives, per_device(): lax.psum((local_weight, local_bias), ('row', 'col'))  100 us
    reduce_scatter x1, waiting for transfers between devices, per_device(): lax.psum_scatter(partial_value.astype(jnp.bfloat16), 'col', scatter_dimen...  86.8 us
    all_gather x1, waiting for transfers between devices, per_device(): grad_block = lax.all_gather(grad_pre, 'col', axis=0, tiled=True)  61.8 us
    scatter-add x1, other arithmetic, per_device(): jax.ops.segment_sum(back_products, slot_cols, num_segments=col_segments)  26.7 us
    scatter-add x1, other arithmetic, per_device(): jax.ops.segment_sum(products, slot_rows, num_segments=row_segments)  17.1 us
  transfers between devices with their start and end apart: 5, of which 5 were waited for; matrix products, arithmetic and copies ran while one was open for 6% of the time, Pallas kernels for 0%

commit v1 on v0

v1 whole, which is shorter than its diff:
```python
import functools

import jax
import jax.numpy as jnp
from jax import lax
from jax.experimental import pallas as pl
from jax.experimental.pallas import tpu as pltpu
from jax.sharding import PartitionSpec as P

MESH = pl.DeviceIdType.MESH
F32 = jnp.float32
BF16 = jnp.bfloat16

Z, YL, X, YH, CORE = 8, 4, 4, 2, 2
ROWS, COLS = Z * YL, X * YH * CORE
TILE = 128
NODE = 256
WIDTH = 128
HID = 256
SLOTS = 128
ROW_TILES = COLS * NODE // TILE
COL_TILES = ROWS * NODE // TILE
SPLIT = 192
REST = NODE - SPLIT
VMEM_LIMIT = 56 * 1024 * 1024


def row_of(z, y):
    return z * YL + y


def col_of(x, yh, core):
    return (x * YH + yh) * CORE + core


def where_am_i():
    row = lax.axis_index("row")
    col = lax.axis_index("col")
    return row, col, row // YL, row % YL, col // (YH * CORE), (col // CORE) % YH, col % CORE


def greet(peers):
    barrier = pltpu.get_barrier_semaphore()
    for peer in peers:
        pl.semaphore_signal(barrier, inc=1, device_id=peer, device_id_type=MESH)
    pl.semaphore_wait(barrier, len(peers))


class Sender:
    def __init__(self, sems):
        self.sems = sems
        self.started = []

    def send(self, src, dst, recv_sem, peer):
        copy = pltpu.make_async_remote_copy(
            src_ref=src,
            dst_ref=dst,
            send_sem=self.sems.at[len(self.started)],
            recv_sem=recv_sem,
            device_id=peer,
            device_id_type=MESH,
        )
        copy.start()
        self.started.append(copy)

    def finish(self):
        for copy in self.started:
            copy.wait_send()


def arrived(dst, recv_sem, peer):
    pltpu.make_async_remote_copy(
        src_ref=dst, dst_ref=dst, send_sem=recv_sem, recv_sem=recv_sem, device_id=peer, device_id_type=MESH
    ).wait_recv()


GATHER_SENDS = 3 + 28 + 7 + 24


def gather_row_kernel(feat, panel, sends, recv_a, recv_b):
    row, col, z, y, _, _, _ = where_am_i()
    up = (row_of((z + 1) % Z, y), col)
    down = (row_of((z + Z - 1) % Z, y), col)
    near = [(row_of(z, (y + j) % YL), col) for j in range(1, YL)]
    greet([up, down] + near)
    out = Sender(sends)
    part_a, part_b = pl.ds(0, SPLIT), pl.ds(SPLIT, REST)

    def shard(dz, j):
        return row_of((z + Z + dz) % Z, (y + j) % YL)

    def a(s):
        return panel.at[s, part_a], recv_a.at[s]

    def b(s):
        return panel.at[s, part_b], recv_b.at[s]

    def pass_on(src, s, way, peer):
        dst, sem = way(s)
        out.send(src, dst, sem, peer)

    mine = feat.at[part_a], feat.at[part_b]
    pass_on(mine[1], row, b, up)
    pass_on(mine[1], row, b, down)
    for j in range(1, YL):
        pass_on(mine[0], row, a, near[j - 1])
    pass_on(mine[0], row, a, up)
    pass_on(mine[0], row, a, down)
    for j in range(1, YL):
        pass_on(mine[1], row, b, near[j - 1])
    panel[row] = feat[...]
    for j in range(1, YL):
        s = shard(0, j)
        arrived(*a(s), near[j - 1])
        pass_on(a(s)[0], s, a, up)
        pass_on(a(s)[0], s, a, down)
    for d in range(1, Z // 2):
        for sign, source, target in ((-1, down, up), (1, up, down)):
            s = shard(sign * d, 0)
            arrived(*b(s), source)
            if d < Z // 2 - 1 or sign < 0:
                pass_on(b(s)[0], s, b, target)
            for j in range(1, YL):
                pass_on(b(s)[0], s, b, near[j - 1])
        for j in range(YL):
            for sign, source, target in ((-1, down, up), (1, up, down)):
                s = shard(sign * d, j)
                arrived(*a(s), source)
                if d < Z // 2 - 1 or (j < 2) == (sign < 0):
                    pass_on(a(s)[0], s, a, target)
    s = shard(Z // 2, 0)
    arrived(*b(s), down)
    for j in range(1, YL):
        pass_on(b(s)[0], s, b, near[j - 1])
    for j in range(YL):
        arrived(*a(shard(Z // 2, j)), down if j < 2 else up)
    for dz in range(Z):
        for j in range(1, YL):
            arrived(*b(shard(dz, j)), near[j - 1])
    out.finish()


def gather_row(features):
    return pl.pallas_call(
        gather_row_kernel,
        out_shape=jax.ShapeDtypeStruct((ROWS, NODE, WIDTH), BF16),
        in_specs=[pl.BlockSpec(memory_space=pltpu.VMEM)],
        out_specs=pl.BlockSpec(memory_space=pltpu.VMEM),
        scratch_shapes=[
            pltpu.SemaphoreType.DMA((GATHER_SENDS,)),
            pltpu.SemaphoreType.DMA((ROWS,)),
            pltpu.SemaphoreType.DMA((ROWS,)),
        ],
        compiler_params=pltpu.CompilerParams(
            collective_id=0, has_side_effects=True, vmem_limit_bytes=VMEM_LIMIT
        ),
    )(features)


STEP = 16
UNROLL = 8


def tiles_kernel(transposed, n_out, pick, place, count, values, panel, out, total):
    step = pl.program_id(0)

    @pl.when(step == 0)
    def _():
        total[...] = jnp.zeros_like(total)

    live = count[0]

    @pl.when(step * STEP < live)
    def _():
        def group(g, carry):
            for u in range(UNROLL):
                k = g * UNROLL + u
                slot = step * STEP + k
                here = panel[pick[slot]]
                dims = (((0,), (0,)), ((), ())) if transposed else (((1,), (0,)), ((), ()))
                product = lax.dot_general(values[k], here, dims, preferred_element_type=F32)
                at = jnp.where(slot < live, place[slot], n_out)
                total[at] += product
            return carry

        lax.fori_loop(0, STEP // UNROLL, group, 0)

    @pl.when(step == SLOTS // STEP - 1)
    def _():
        out[...] = total[:n_out].astype(BF16)


def tile_products(values, pick, place, count, panel, n_out, transposed):
    n_in = panel.shape[0]
    return pl.pallas_call(
        functools.partial(tiles_kernel, transposed, n_out),
        out_shape=jax.ShapeDtypeStruct((n_out, TILE, WIDTH), BF16),
        grid_spec=pltpu.PrefetchScalarGridSpec(
            num_scalar_prefetch=3,
            grid=(SLOTS // STEP,),
            in_specs=[
                pl.BlockSpec((STEP, TILE, TILE), lambda i, *_: (i, 0, 0)),
                pl.BlockSpec((n_in, TILE, WIDTH), lambda i, *_: (0, 0, 0)),
            ],
            out_specs=pl.BlockSpec((n_out, TILE, WIDTH), lambda i, *_: (0, 0, 0)),
            scratch_shapes=[pltpu.VMEM((n_out + 1, TILE, WIDTH), F32)],
        ),
        compiler_params=pltpu.CompilerParams(
            dimension_semantics=("arbitrary",), vmem_limit_bytes=VMEM_LIMIT
        ),
    )(pick, place, count, values, panel)


MIDDLE_SENDS = 4 + 3 + 1 + 1 + 6 + 8


def middle_kernel(
    partial, grad_out, weight, bias, hidden, block, gw, gb,
    paired, pair_in, x_in, y_out, y_in, sends, pair_sem, x_sem, y_sem, gather_sem,
):
    row, col, _, _, x, yh, core = where_am_i()
    sibling = (row, col_of(x, yh, 1 - core))
    far = (row, col_of(x, 1 - yh, core))
    ring = [(row, col_of((x + d) % X, yh, core)) for d in range(1, X)]
    greet([sibling, far] + ring)
    out = Sender(sends)
    order = [2, 1, 3, 0]
    for d in order:
        other = (x + d) % X
        out.send(partial.at[other, :, 1 - core], pair_in.at[d], pair_sem.at[d], sibling)
    for d in order:
        other = (x + d) % X
        arrived(pair_in.at[d], pair_sem.at[d], sibling)
        for h in range(YH):
            paired[d, h] = (partial[other, h, core].astype(F32) + pair_in[d, h].astype(F32)).astype(BF16)
        if d:
            out.send(paired.at[d], x_in.at[X - d], x_sem.at[X - d], ring[d - 1])
    for d in range(1, X):
        arrived(x_in.at[d], x_sem.at[d], ring[d - 1])

    def summed(h):
        acc = paired[0, h].astype(F32)
        for d in range(1, X):
            acc += x_in[d, h].astype(F32)
        return acc

    y_out[...] = summed(1 - yh).astype(BF16)
    out.send(y_out, y_in, y_sem.at[0], far)
    own = summed(yh)
    arrived(y_in, y_sem.at[0], far)
    aggregate = (own + y_in[...].astype(F32)).astype(BF16)
    preact = jnp.dot(aggregate, weight[...], preferred_element_type=F32) + bias[...]
    sigmoid = jax.nn.sigmoid(preact)
    slope = sigmoid * (1.0 + preact * (1.0 - sigmoid))
    grad_pre = (grad_out[...].astype(F32) * slope).astype(BF16)
    block[col] = lax.dot_general(
        grad_pre, weight[...], (((1,), (1,)), ((), ())), preferred_element_type=F32
    ).astype(BF16)

    def g(c):
        return block.at[c], gather_sem.at[c]

    def pass_on(c, peer):
        out.send(block.at[c], block.at[c], gather_sem.at[c], peer)

    pass_on(col, far)
    for d in order[:3]:
        pass_on(col, ring[d - 1])
    pass_on(col, sibling)
    hidden[...] = (preact * sigmoid).astype(BF16)
    gw[...] = lax.dot_general(aggregate, grad_pre, (((0,), (0,)), ((), ())), preferred_element_type=F32)
    gb[...] = jnp.broadcast_to(jnp.sum(grad_pre.astype(F32), axis=0, keepdims=True), gb.shape)
    c = col_of(x, 1 - yh, core)
    arrived(*g(c), far)
    for d in order[:3]:
        pass_on(c, ring[d - 1])
    pass_on(c, sibling)
    for d in (1, 3, 2):
        for h in (yh, 1 - yh):
            c = col_of((x + d) % X, h, core)
            arrived(*g(c), ring[d - 1])
            pass_on(c, sibling)
    for d in range(X):
        for h in range(YH):
            arrived(*g(col_of((x + d) % X, h, 1 - core)), sibling)
    out.finish()


def middle(partial, grad_out, weight, bias):
    return pl.pallas_call(
        middle_kernel,
        out_shape=(
            jax.ShapeDtypeStruct((NODE, HID), BF16),
            jax.ShapeDtypeStruct((COLS, NODE, WIDTH), BF16),
            jax.ShapeDtypeStruct((WIDTH, HID), F32),
            jax.ShapeDtypeStruct((8, HID), F32),
        ),
        in_specs=[pl.BlockSpec(memory_space=pltpu.VMEM)] * 4,
        out_specs=(pl.BlockSpec(memory_space=pltpu.VMEM),) * 4,
        scratch_shapes=[
            pltpu.VMEM((X, YH, NODE, WIDTH), BF16),
            pltpu.VMEM((X, YH, NODE, WIDTH), BF16),
            pltpu.VMEM((X, YH, NODE, WIDTH), BF16),
            pltpu.VMEM((NODE, WIDTH), BF16),
            pltpu.VMEM((NODE, WIDTH), BF16),
            pltpu.SemaphoreType.DMA((MIDDLE_SENDS,)),
            pltpu.SemaphoreType.DMA((X,)),
            pltpu.SemaphoreType.DMA((X,)),
            pltpu.SemaphoreType.DMA((1,)),
            pltpu.SemaphoreType.DMA((COLS,)),
        ],
        compiler_params=pltpu.CompilerParams(
            collective_id=1, has_side_effects=True, vmem_limit_bytes=VMEM_LIMIT
        ),
    )(partial, grad_out, weight, bias)


PIECE = WIDTH // COLS
SCATTER_SENDS = 3 + 7 + 28 + 3 + (COLS - 1) * 2 + 3 + 7


def scatter_row_kernel(
    partial, gw, gb, result, gw_out, gb_out,
    a_out, a_in, near_out, near_in, b_first, b_sum, b_out, b_in,
    piece, piece_in, near_piece, far_piece, near_piece_in, far_piece_in,
    sends, a_sem, near_sem, b_first_sem, b_sem, piece_sem, np_sem, fp_sem, last_sem,
):
    row, col, z, y, _, _, _ = where_am_i()
    up = (row_of((z + 1) % Z, y), col)
    down = (row_of((z + Z - 1) % Z, y), col)
    near = [(row_of(z, (y + j) % YL), col) for j in range(1, YL)]
    along = [(row_of((z + d) % Z, y), col) for d in range(1, Z)]
    across = [(row, (col + d) % COLS) for d in range(1, COLS)]
    greet(near + along + across)
    out = Sender(sends)
    part_a, part_b = pl.ds(0, SPLIT), pl.ds(SPLIT, REST)
    half = Z // 2
    ways = ((0, 1, up, down), (1, -1, down, up))

    def own_a(dz, j):
        return partial.at[(z + Z + dz) % Z, (y + j) % YL, part_a]

    for j in range(1, YL):
        out.send(partial.at[:, (y + j) % YL, part_b], b_first.at[YL - j], b_first_sem.at[YL - j], near[j - 1])
    for j in (1, 2, 3, 0):
        way, sign, target, _ = ways[0] if j < 2 else ways[1]
        out.send(own_a(half, j), a_in.at[way, 0, j], a_sem.at[way, 0, j], target)
    for j in (1, 2, 3, 0):
        way, sign, target, _ = ways[1] if j < 2 else ways[0]
        out.send(own_a(sign * (half - 1), j), a_in.at[way, 1, j], a_sem.at[way, 1, j], target)

    for p in range(COLS):
        piece[p, 0:PIECE] = gw[p * PIECE:(p + 1) * PIECE]
        piece[p, PIECE:] = gb[...]
    for d in range(1, COLS):
        to = (col + d) % COLS
        out.send(piece.at[to], piece_in.at[COLS - d], piece_sem.at[COLS - d], across[d - 1])

    for j in (1, 2, 3, 0):
        way, sign, target, source = ways[0] if j < 2 else ways[1]
        arrived(a_in.at[way, 0, j], a_sem.at[way, 0, j], source)
        a_out[way, 1, j] = (own_a(sign * (half - 1), j)[...].astype(F32) + a_in[way, 0, j].astype(F32)).astype(BF16)
        out.send(a_out.at[way, 1, j], a_in.at[way, 1, j], a_sem.at[way, 1, j], target)

    for j in range(1, YL):
        arrived(b_first.at[j], b_first_sem.at[j], near[j - 1])
    for dz in range(Z):
        at = (z + dz) % Z
        acc = partial[at, y, SPLIT:].astype(F32)
        for j in range(1, YL):
            acc += b_first[j, at].astype(F32)
        b_sum[dz] = acc

    def rest_step(step):
        for way, sign, target, source in ways:
            if step == 0 and way == 1:
                continue
            acc = b_sum[(sign * (half - step)) % Z]
            if step > (0 if way == 0 else 1):
                arrived(b_in.at[way, step - 1], b_sem.at[way, step - 1], source)
                acc = acc + b_in[way, step - 1].astype(F32)
            b_out[way, step] = acc.astype(BF16)
            out.send(b_out.at[way, step], b_in.at[way, step], b_sem.at[way, step], target)

    rest_step(0)
    for step in (2, 3):
        for j in (1, 2, 3, 0):
            for way, sign, target, source in ways:
                arrived(a_in.at[way, step - 1, j], a_sem.at[way, step - 1, j], source)
                a_out[way, step, j] = (
                    own_a(sign * (half - step), j)[...].astype(F32) + a_in[way, step - 1, j].astype(F32)
                ).astype(BF16)
                out.send(a_out.at[way, step, j], a_in.at[way, step, j], a_sem.at[way, step, j], target)
        rest_step(step - 1)
        if step == 2:
            acc = piece[col]
            for d in range(1, COLS):
                arrived(piece_in.at[d], piece_sem.at[d], across[d - 1])
                acc = acc + piece_in[d]
            near_piece[...] = acc
            for j in range(1, YL):
                out.send(near_piece, near_piece_in.at[YL - j], np_sem.at[YL - j], near[j - 1])
        else:
            acc = near_piece[...]
            for j in range(1, YL):
                arrived(near_piece_in.at[j], np_sem.at[j], near[j - 1])
                acc = acc + near_piece_in[j]
            far_piece[...] = acc
            for d in range(1, Z):
                out.send(far_piece, far_piece_in.at[Z - d], fp_sem.at[Z - d], along[d - 1])
    rest_step(3)

    def final_a(j):
        acc = own_a(0, j)[...].astype(F32)
        for way, _, _, source in ways:
            arrived(a_in.at[way, 3, j], a_sem.at[way, 3, j], source)
            acc += a_in[way, 3, j].astype(F32)
        return acc

    for j in range(1, YL):
        near_out[j] = final_a(j).astype(BF16)
        out.send(near_out.at[j], near_in.at[YL - j], near_sem.at[YL - j], near[j - 1])
    mine = final_a(0)

    acc = far_piece[...]
    for d in range(1, Z):
        arrived(far_piece_in.at[d], fp_sem.at[d], along[d - 1])
        acc = acc + far_piece_in[d]
    gw_out[col] = acc[0:PIECE]
    gb_out[...] = acc[PIECE:]
    for d in range(1, COLS):
        out.send(gw_out.at[col], gw_out.at[col], last_sem.at[col], across[d - 1])

    acc = b_sum[0]
    for way, _, _, source in ways:
        arrived(b_in.at[way, 3], b_sem.at[way, 3], source)
        acc = acc + b_in[way, 3].astype(F32)
    result[SPLIT:] = acc.astype(BF16)
    for j in range(1, YL):
        arrived(near_in.at[j], near_sem.at[j], near[j - 1])
        mine += near_in[j].astype(F32)
    result[:SPLIT] = mine.astype(BF16)
    for d in range(1, COLS):
        at = (col + d) % COLS
        arrived(gw_out.at[at], last_sem.at[at], across[d - 1])
    out.finish()


def scatter_row(partial, gw, gb):
    return pl.pallas_call(
        scatter_row_kernel,
        out_shape=(
            jax.ShapeDtypeStruct((NODE, WIDTH), BF16),
            jax.ShapeDtypeStruct((COLS, PIECE, HID), F32),
            jax.ShapeDtypeStruct((8, HID), F32),
        ),
        in_specs=[pl.BlockSpec(memory_space=pltpu.VMEM)] * 3,
        out_specs=(pl.BlockSpec(memory_space=pltpu.VMEM),) * 3,
        scratch_shapes=[
            pltpu.VMEM((2, 4, YL, SPLIT, WIDTH), BF16),
            pltpu.VMEM((2, 4, YL, SPLIT, WIDTH), BF16),
            pltpu.VMEM((YL, SPLIT, WIDTH), BF16),
            pltpu.VMEM((YL, SPLIT, WIDTH), BF16),
            pltpu.VMEM((YL, Z, REST, WIDTH), BF16),
            pltpu.VMEM((Z, REST, WIDTH), F32),
            pltpu.VMEM((2, 4, REST, WIDTH), BF16),
            pltpu.VMEM((2, 4, REST, WIDTH), BF16),
            pltpu.VMEM((COLS, PIECE + 8, HID), F32),
            pltpu.VMEM((COLS, PIECE + 8, HID), F32),
            pltpu.VMEM((PIECE + 8, HID), F32),
            pltpu.VMEM((PIECE + 8, HID), F32),
            pltpu.VMEM((YL, PIECE + 8, HID), F32),
            pltpu.VMEM((Z, PIECE + 8, HID), F32),
            pltpu.SemaphoreType.DMA((SCATTER_SENDS,)),
            pltpu.SemaphoreType.DMA((2, 4, YL)),
            pltpu.SemaphoreType.DMA((YL,)),
            pltpu.SemaphoreType.DMA((YL,)),
            pltpu.SemaphoreType.DMA((2, 4)),
            pltpu.SemaphoreType.DMA((COLS,)),
            pltpu.SemaphoreType.DMA((YL,)),
            pltpu.SemaphoreType.DMA((Z,)),
            pltpu.SemaphoreType.DMA((COLS,)),
        ],
        compiler_params=pltpu.CompilerParams(
            collective_id=2, has_side_effects=True, vmem_limit_bytes=VMEM_LIMIT
        ),
    )(partial, gw, gb)


def per_device(features, weight, bias, grad_out, tile_values, tile_rows, tile_cols, tile_count):
    values = tile_values[0, 0]
    slot_rows = tile_rows[0, 0]
    slot_cols = tile_cols[0, 0]
    count = tile_count.reshape(1)
    panel = gather_row(features).reshape(COL_TILES, TILE, WIDTH)
    partial = tile_products(values, slot_cols, slot_rows, count, panel, ROW_TILES, False)
    hidden, block, gw, gb = middle(
        partial.reshape(X, YH, CORE, NODE, WIDTH), grad_out, weight, bias.reshape(1, HID)
    )
    back = tile_products(
        values, slot_rows, slot_cols, count, block.reshape(ROW_TILES, TILE, WIDTH), COL_TILES, True
    )
    grad_features, grad_weight, grad_bias = scatter_row(back.reshape(Z, YL, NODE, WIDTH), gw, gb)
    return hidden, grad_weight.reshape(WIDTH, HID), grad_bias[0], grad_features


def solution(mesh):
    return jax.shard_map(
        per_device,
        mesh=mesh,
        in_specs=(
            P(("col", "row"), None),
            P(),
            P(),
            P(("row", "col"), None),
            P("row", "col", None, None, None),
            P("row", "col", None),
            P("row", "col", None),
            P("row", "col"),
        ),
        out_specs=(P(("row", "col"), None), P(), P(), P(("col", "row"), None)),
        check_vma=False,
    )
```

time: 796 us -> 150 us (0.19)
  the two profiles are of different devices: /device:TPU:6 before, /device:TPU:1 now
where the time goes in v1:
time: 150 us; the launch traced here: 147 us
  Pallas kernels  141 us (94%)
  local copies, waits for them, and re-layouts  4.96 us (3%)
    pallas_call x1, Pallas kernels, scatter_row(): pl.pallas_call(scatter_row_kernel, out_shape=(jax.ShapeDtypeStruct((NODE,...  46.7 us
    pallas_call x1, Pallas kernels, gather_row(): pl.pallas_call(gather_row_kernel, out_shape=jax.ShapeDtypeStruct((ROWS, N...  38.2 us
    pallas_call x1, Pallas kernels, middle(): pl.pallas_call(middle_kernel, out_shape=(jax.ShapeDtypeStruct((NODE, HID)...  37.5 us
    pallas_call x2, Pallas kernels, tile_products(): pl.pallas_call(functools.partial(tiles_kernel, transposed, n_out), out_sh...  18.3 us
    unnamed x5, local copies, waits for them, and re-layouts  3.7 us

profile of v1, /device:TPU:1, one launch (start us, length us, event | category | flops | bytes accessed | tf_op | source)
XLA Modules:
  0.0 146.9 jit_solution(2175356501385725593)
XLA Ops:
  1.3 38.2 %shard_map.111 = bf16[32,256,128]{2,1,0:T(8,128)(2,1)} custom-call(bf16[256,128]{1,0:T(8,128)(2,1)} %feat.1), custom_call_target="tpu_custom_call" | custom-call | tf_op jit(solution)/shard_map/pallas_call | solution.py:144
  39.4 8.9 %shard_map.112 = bf16[32,128,128]{2,1,0:T(8,128)(2,1)} custom-call(s32[128]{0:T(128)} %bitcast.20, s32[128]{0:T(128)} %bitcast.22, s32[1]{0:T(128)} %bitcast.11.count, bf16[128,128,128]{2,1,0:T(8,128)(2,1)} %bitcast.13, bf16[64,128,128]{2,1,0:T(8,128)(2,1)} %bitcast.16), custom_call_target="tpu_custom_call" | custom-call | tf_op jit(solution)/shard_map/pallas_call | solution.py:195
  48.3 37.5 %shard_map.113 = (bf16[256,256]{1,0:T(8,128)(2,1)}, bf16[16,256,128]{2,1,0:T(8,128)(2,1)}, f32[128,256]{1,0:T(8,128)}, f32[8,256]{1,0:T(8,128)}) custom-call(bf16[4,2,2,256,128]{4,3,2,1,0:T(8,128)(2,1)} %bitcast.17, bf16[256,256]{1,0:T(8,128)(2,1)} %grad_out.1, bf16[128,256]{1,0:T(8,128)(2,1)} %weight.1, f32[1,256]{1,0:T(1,128)} %bitcast.25), custom_call_target="tpu_custom_call" | custom-call | tf_op jit(solution)/shard_map/pallas_call | solution.py:290
  85.8 9.4 %shard_map.114 = bf16[64,128,128]{2,1,0:T(8,128)(2,1)} custom-call(s32[128]{0:T(128)} %bitcast.23, s32[128]{0:T(128)} %bitcast.21, s32[1]{0:T(128)} %bitcast.12.count, bf16[128,128,128]{2,1,0:T(8,128)(2,1)} %bitcast.14, bf16[32,128,128]{2,1,0:T(8,128)(2,1)} %bitcast.18), custom_call_target="tpu_custom_call" | custom-call | tf_op jit(solution)/shard_map/pallas_call | solution.py:195
  95.2 0.0 copy-start
  95.2 46.7 %shard_map.115 = (bf16[256,128]{1,0:T(8,128)(2,1)}, f32[16,8,256]{2,1,0:T(8,128)}, f32[8,256]{1,0:T(8,128)}) custom-call(bf16[8,4,256,128]{3,2,1,0:T(8,128)(2,1)} %bitcast.15, f32[128,256]{1,0:T(8,128)} %get-tuple-element.13.gw, f32[8,256]{1,0:T(8,128)} %get-tuple-element.14.gb), custom_call_target="tpu_custom_call" | custom-call | tf_op jit(solution)/shard_map/pallas_call | solution.py:450
  142.0 1.3 slice.3
  143.2 0.0 copy-done
  143.3 0.7 copy.16
  143.9 1.6 %copy.17 = f32[128,256]{1,0:T(8,128)} copy(f32[128,256]{1,0:T(8,128)} %bitcast.19) | data formatting | bytes 262144
  145.5 1.5 %copy.18 = bf16[256,128]{1,0:T(8,128)(2,1)} copy(bf16[256,128]{1,0:T(8,128)(2,1)} %get-tuple-element.25) | data formatting | bytes 131072
Async XLA Ops:
  95.2 48.0 %copy-start = (bf16[256,256]{1,0:T(8,128)(2,1)S(1)}, bf16[256,256]{1,0:T(8,128)(2,1)}, u32[]{:S(2)}) copy-start(bf16[256,256]{1,0:T(8,128)(2,1)} %get-tuple-element.22) | copy-start | bytes 393220

commit v2 on v0

v2 whole, which is shorter than its diff:
```python
import functools

import jax
import jax.numpy as jnp
from jax import lax
from jax.experimental import pallas as pl
from jax.experimental.pallas import tpu as pltpu
from jax.sharding import PartitionSpec as P

MESH = pl.DeviceIdType.MESH
F32 = jnp.float32
BF16 = jnp.bfloat16

Z, YL, X, YH, CORE = 8, 4, 4, 2, 2
ROWS, COLS = Z * YL, X * YH * CORE
TILE = 128
NODE = 256
WIDTH = 128
HID = 256
SLOTS = 128
ROW_TILES = COLS * NODE // TILE
COL_TILES = ROWS * NODE // TILE
SPLIT = 192
REST = NODE - SPLIT
VMEM_LIMIT = 56 * 1024 * 1024


def row_of(z, y):
    return z * YL + y


def col_of(x, yh, core):
    return (x * YH + yh) * CORE + core


def where_am_i():
    row = lax.axis_index("row")
    col = lax.axis_index("col")
    return row, col, row // YL, row % YL, col // (YH * CORE), (col // CORE) % YH, col % CORE


def greet(peers):
    barrier = pltpu.get_barrier_semaphore()
    for peer in peers:
        pl.semaphore_signal(barrier, inc=1, device_id=peer, device_id_type=MESH)
    pl.semaphore_wait(barrier, len(peers))


class Sender:
    def __init__(self, sems):
        self.sems = sems
        self.started = []

    def send(self, src, dst, recv_sem, peer):
        copy = pltpu.make_async_remote_copy(
            src_ref=src,
            dst_ref=dst,
            send_sem=self.sems.at[len(self.started)],
            recv_sem=recv_sem,
            device_id=peer,
            device_id_type=MESH,
        )
        copy.start()
        self.started.append(copy)

    def finish(self):
        for copy in self.started:
            copy.wait_send()


def arrived(dst, recv_sem, peer):
    pltpu.make_async_remote_copy(
        src_ref=dst, dst_ref=dst, send_sem=recv_sem, recv_sem=recv_sem, device_id=peer, device_id_type=MESH
    ).wait_recv()


HALF_Z = Z // 2
PIECES = 16
PIECE = WIDTH // PIECES
EXTRA = 8
UNROLL = 16
GATHER_SENDS = 3 + 28 + 7 + 24
MIDDLE_SENDS = 8 + 6 + 1 + 1 + 6 + 8
PARAM_SENDS = 1 + 3 + 1 + 3 + 7 + 1 + 6 + 8
SCATTER_SENDS = 28 + 3
SENDS = GATHER_SENDS + MIDDLE_SENDS + PARAM_SENDS + SCATTER_SENDS


def dot(a, b, ca, cb):
    return lax.dot_general(a, b, (((ca,), (cb,)), ((), ())), preferred_element_type=F32)


def plan(segment, pick, live, last_tile):
    n = SLOTS
    lane = lax.broadcasted_iota(jnp.int32, (n, n), 1)
    sub = lax.broadcasted_iota(jnp.int32, (n, n), 0)
    seg = jnp.where(live, segment, last_tile)
    seg_l = jnp.broadcast_to(seg, (n, n))
    seg_s = seg_l.T
    key_l = seg_l * n + lane
    key_s = seg_s * n + sub
    rank = jnp.sum((key_s < key_l).astype(jnp.int32), axis=0, keepdims=True)
    rank_s = jnp.broadcast_to(rank, (n, n)).T
    hot = (rank_s == lane).astype(jnp.int32)
    pick_s = jnp.broadcast_to(pick, (n, n)).T
    order = jnp.sum(hot * sub, axis=0, keepdims=True)
    picked = jnp.sum(hot * pick_s, axis=0, keepdims=True)
    placed = jnp.sum(hot * seg_s, axis=0, keepdims=True)
    before = jnp.sum((rank_s == lane - 1).astype(jnp.int32) * seg_s, axis=0, keepdims=True)
    keep = jnp.where((placed == before) & (lane[0:1] > 0), 1.0, 0.0)
    upto = jnp.sum((seg_s <= lane).astype(jnp.int32), axis=0, keepdims=True)
    exact = jnp.sum((seg_s == lane).astype(jnp.int32), axis=0, keepdims=True)
    last = jnp.maximum(upto - 1, 0)
    has = jnp.where(exact > 0, 1.0, 0.0)
    return order, picked, last, keep, has


def products(base, ints, floats, values, panel, run, contract):
    def group(g, acc):
        for u in range(UNROLL):
            i = g * UNROLL + u
            slot, tile = ints[base, i], ints[base + 1, i]
            acc = acc * floats[base, i] + dot(values[slot], panel[tile], contract, 0)
            run[i] = acc.astype(BF16)
        return acc

    lax.fori_loop(0, SLOTS // UNROLL, group, jnp.zeros((TILE, WIDTH), F32))


def whole_kernel(
    feat, weight, bias, grad_out, values_hbm, rows_ref, cols_ref, count_ref,
    hidden, gw_out, gb_out, result,
    values, panel, run, partial, paired, pair_in, x_in, y_out, y_in, block, back,
    a_out, a_in, near_out, near_in,
    core_piece, core_piece_in, x_piece, x_piece_in, far_piece, far_piece_in, near_piece, near_piece_in, z_piece, z_piece_in,
    ints_v, floats_v, ints, floats,
    sends, values_sem, table_sem, recv_a, recv_b, pair_sem, x_sem, y_sem, gather_sem, a_sem, near_sem,
    core_psem, x_psem, far_psem, near_psem, z_psem, last_sem,
):
    row, col, z, y, x, yh, core = where_am_i()
    load = pltpu.make_async_copy(values_hbm, values, values_sem)
    load.start()
    up = (row_of((z + 1) % Z, y), col)
    down = (row_of((z + Z - 1) % Z, y), col)
    near = [(row_of(z, (y + j) % YL), col) for j in range(1, YL)]
    along = [(row_of((z + d) % Z, y), col) for d in range(1, Z)]
    sibling = (row, col_of(x, yh, 1 - core))
    far = (row, col_of(x, 1 - yh, core))
    ring = [(row, col_of((x + d) % X, yh, core)) for d in range(1, X)]
    greet(near + along + [sibling, far] + ring)
    out = Sender(sends)

    part_a, part_b = pl.ds(0, SPLIT), pl.ds(SPLIT, REST)

    def shard(dz, j):
        return row_of((z + Z + dz) % Z, (y + j) % YL)

    def a(s):
        return panel.at[s, part_a], recv_a.at[s]

    def b(s):
        return panel.at[s, part_b], recv_b.at[s]

    def pass_on(src, s, way, peer):
        dst, sem = way(s)
        out.send(src, dst, sem, peer)

    mine = feat.at[part_a], feat.at[part_b]
    pass_on(mine[1], row, b, up)
    pass_on(mine[1], row, b, down)
    for j in range(1, YL):
        pass_on(mine[0], row, a, near[j - 1])
    pass_on(mine[0], row, a, up)
    pass_on(mine[0], row, a, down)
    for j in range(1, YL):
        pass_on(mine[1], row, b, near[j - 1])
    panel[row] = feat[...]

    live = lax.broadcasted_iota(jnp.int32, (1, SLOTS), 1) < count_ref[...]
    ints_v[...] = jnp.zeros_like(ints_v)
    floats_v[...] = jnp.zeros_like(floats_v)
    for base, segment, pick, tiles in ((0, rows_ref, cols_ref, ROW_TILES), (3, cols_ref, rows_ref, COL_TILES)):
        order, picked, last, keep, has = plan(segment[...], pick[...], live, tiles)
        ints_v[base:base + 1] = order
        ints_v[base + 1:base + 2] = picked
        ints_v[base + 2:base + 3] = last
        floats_v[base:base + 1] = keep
        floats_v[base + 2:base + 3] = has
    table = [
        pltpu.make_async_copy(ints_v, ints, table_sem.at[0]),
        pltpu.make_async_copy(floats_v, floats, table_sem.at[1]),
    ]
    for copy in table:
        copy.start()

    for j in range(1, YL):
        s = shard(0, j)
        arrived(*a(s), near[j - 1])
        pass_on(a(s)[0], s, a, up)
        pass_on(a(s)[0], s, a, down)
    for d in range(1, HALF_Z):
        for sign, source, target in ((-1, down, up), (1, up, down)):
            s = shard(sign * d, 0)
            arrived(*b(s), source)
            if d < HALF_Z - 1 or sign < 0:
                pass_on(b(s)[0], s, b, target)
            for j in range(1, YL):
                pass_on(b(s)[0], s, b, near[j - 1])
        for j in range(YL):
            for sign, source, target in ((-1, down, up), (1, up, down)):
                s = shard(sign * d, j)
                arrived(*a(s), source)
                if d < HALF_Z - 1 or (j < 2) == (sign < 0):
                    pass_on(a(s)[0], s, a, target)
    s = shard(HALF_Z, 0)
    arrived(*b(s), down)
    for j in range(1, YL):
        pass_on(b(s)[0], s, b, near[j - 1])
    for copy in table:
        copy.wait()
    load.wait()
    for j in range(YL):
        arrived(*a(shard(HALF_Z, j)), down if j < 2 else up)
    for dz in range(Z):
        for j in range(1, YL):
            arrived(*b(shard(dz, j)), near[j - 1])

    products(0, ints, floats, values, panel.reshape(COL_TILES, TILE, WIDTH), run, 1)
    tiles_per = NODE // TILE
    for r in range(ROW_TILES):
        c, t = r // tiles_per, r % tiles_per
        tile = (run[ints[2, r]].astype(F32) * floats[2, r]).astype(BF16)
        partial[c // (YH * CORE), (c // CORE) % YH, c % CORE, t * TILE:(t + 1) * TILE] = tile

    order = [2, 1, 3, 0]
    for h in range(YH):
        hh = (1 - yh) if h == 0 else yh
        for d in order:
            other = (x + d) % X
            out.send(partial.at[other, hh, 1 - core], pair_in.at[h, d], pair_sem.at[h, d], sibling)
    for h in range(YH):
        hh = (1 - yh) if h == 0 else yh
        for d in order:
            other = (x + d) % X
            arrived(pair_in.at[h, d], pair_sem.at[h, d], sibling)
            paired[h, d] = (partial[other, hh, core].astype(F32) + pair_in[h, d].astype(F32)).astype(BF16)
            if d:
                out.send(paired.at[h, d], x_in.at[h, X - d], x_sem.at[h, X - d], ring[d - 1])

    def summed(h):
        acc = paired[h, 0].astype(F32)
        for d in range(1, X):
            arrived(x_in.at[h, d], x_sem.at[h, d], ring[d - 1])
            acc += x_in[h, d].astype(F32)
        return acc

    y_out[...] = summed(0).astype(BF16)
    out.send(y_out, y_in, y_sem.at[0], far)
    own = summed(1)
    arrived(y_in, y_sem.at[0], far)
    aggregate = (own + y_in[...].astype(F32)).astype(BF16)

    preact = jnp.dot(aggregate, weight[...], preferred_element_type=F32) + bias[...]
    sigmoid = jax.nn.sigmoid(preact)
    slope = sigmoid * (1.0 + preact * (1.0 - sigmoid))
    grad_pre = (grad_out[...].astype(F32) * slope).astype(BF16)
    block[col] = dot(grad_pre, weight[...], 1, 1).astype(BF16)

    def g(c):
        return block.at[c], gather_sem.at[c]

    def share(c, peer):
        out.send(block.at[c], block.at[c], gather_sem.at[c], peer)

    share(col, far)
    for d in order[:3]:
        share(col, ring[d - 1])
    share(col, sibling)
    hidden[...] = (preact * sigmoid).astype(BF16)
    gw = dot(aggregate, grad_pre, 0, 0)
    gb = jnp.broadcast_to(jnp.sum(grad_pre.astype(F32), axis=0, keepdims=True), (EXTRA, HID))
    half = WIDTH // CORE
    for c in range(CORE):
        core_piece[c, :half] = gw[c * half:(c + 1) * half]
        core_piece[c, half:] = gb
    out.send(core_piece.at[1 - core], core_piece_in, core_psem.at[0], sibling)
    c = col_of(x, 1 - yh, core)
    arrived(*g(c), far)
    for d in order[:3]:
        share(c, ring[d - 1])
    share(c, sibling)
    arrived(core_piece_in, core_psem.at[0], sibling)
    quarter = half // X
    for q in range(X):
        for here, size, at in ((q * quarter, quarter, 0), (half, EXTRA, quarter)):
            x_piece[q, at:at + size] = core_piece[core, here:here + size] + core_piece_in[here:here + size]
    for d in range(1, X):
        out.send(x_piece.at[(x + d) % X], x_piece_in.at[X - d], x_psem.at[X - d], ring[d - 1])
    for d in (1, 3, 2):
        for h in (yh, 1 - yh):
            c = col_of((x + d) % X, h, core)
            arrived(*g(c), ring[d - 1])
            share(c, sibling)
    acc = x_piece[x]
    for d in range(1, X):
        arrived(x_piece_in.at[d], x_psem.at[d], ring[d - 1])
        acc = acc + x_piece_in[d]
    for h in range(YH):
        far_piece[h, :PIECE] = acc[h * PIECE:(h + 1) * PIECE]
        far_piece[h, PIECE:] = acc[quarter:]
    out.send(far_piece.at[1 - yh], far_piece_in, far_psem.at[0], far)
    for d in range(X):
        for h in range(YH):
            arrived(*g(col_of((x + d) % X, h, 1 - core)), sibling)

    products(3, ints, floats, values, block.reshape(ROW_TILES, TILE, WIDTH), run, 0)
    for r in range(COL_TILES):
        s, t = r // tiles_per, r % tiles_per
        tile = (run[ints[5, r]].astype(F32) * floats[5, r]).astype(BF16)
        back[s // YL, s % YL, t * TILE:(t + 1) * TILE] = tile

    ways = ((0, 1, up, down), (1, -1, down, up))
    turns = (1, 2, 3, 0)

    def own_a(dz, j):
        return back.at[(z + Z + dz) % Z, (y + j) % YL]

    for j in turns:
        way, _, target, _ = ways[0] if j < 2 else ways[1]
        out.send(own_a(HALF_Z, j), a_in.at[way, 0, j], a_sem.at[way, 0, j], target)
    for j in turns:
        way, sign, target, _ = ways[1] if j < 2 else ways[0]
        out.send(own_a(sign * (HALF_Z - 1), j), a_in.at[way, 1, j], a_sem.at[way, 1, j], target)
    arrived(far_piece_in, far_psem.at[0], far)
    near_piece[...] = far_piece[yh] + far_piece_in[...]
    for j in range(1, YL):
        out.send(near_piece, near_piece_in.at[YL - j], near_psem.at[YL - j], near[j - 1])

    def hop(step, j, way, sign, target, source):
        arrived(a_in.at[way, step - 1, j], a_sem.at[way, step - 1, j], source)
        a_out[way, step, j] = (
            own_a(sign * (HALF_Z - step), j)[...].astype(F32) + a_in[way, step - 1, j].astype(F32)
        ).astype(BF16)
        out.send(a_out.at[way, step, j], a_in.at[way, step, j], a_sem.at[way, step, j], target)

    for j in turns:
        hop(1, j, *(ways[0] if j < 2 else ways[1]))
    acc = near_piece[...]
    for j in range(1, YL):
        arrived(near_piece_in.at[j], near_psem.at[j], near[j - 1])
        acc = acc + near_piece_in[j]
    z_piece[...] = acc
    for d in range(1, Z):
        out.send(z_piece, z_piece_in.at[Z - d], z_psem.at[Z - d], along[d - 1])
    for j in turns:
        for way in ways:
            hop(2, j, *way)
    acc = z_piece[...]
    for d in range(1, Z):
        arrived(z_piece_in.at[d], z_psem.at[d], along[d - 1])
        acc = acc + z_piece_in[d]

    def spot(x_at, h, c):
        return (c * X + x_at) * YH + h

    def last(p):
        return gw_out.at[p], last_sem.at[p]

    def spread(p, peer):
        out.send(gw_out.at[p], gw_out.at[p], last_sem.at[p], peer)

    gw_out[spot(x, yh, core)] = acc[:PIECE]
    gb_out[...] = acc[PIECE:]
    spread(spot(x, yh, core), far)
    for d in range(1, X):
        spread(spot(x, yh, core), ring[d - 1])
    spread(spot(x, yh, core), sibling)
    for j in turns:
        for way in ways:
            hop(3, j, *way)
    p = spot(x, 1 - yh, core)
    arrived(*last(p), far)
    for d in range(1, X):
        spread(p, ring[d - 1])
    spread(p, sibling)

    def final_a(j):
        acc = own_a(0, j)[...].astype(F32)
        for way, _, _, source in ways:
            arrived(a_in.at[way, 3, j], a_sem.at[way, 3, j], source)
            acc += a_in[way, 3, j].astype(F32)
        return acc

    for j in range(1, YL):
        near_out[j] = final_a(j).astype(BF16)
        out.send(near_out.at[j], near_in.at[YL - j], near_sem.at[YL - j], near[j - 1])
    for d in range(1, X):
        for h in (yh, 1 - yh):
            p = spot((x + d) % X, h, core)
            arrived(*last(p), ring[d - 1])
            spread(p, sibling)
    total = final_a(0)
    for j in range(1, YL):
        arrived(near_in.at[j], near_sem.at[j], near[j - 1])
        total += near_in[j].astype(F32)
    result[...] = total.astype(BF16)
    for d in range(X):
        for h in range(YH):
            arrived(*last(spot((x + d) % X, h, 1 - core)), sibling)
    out.finish()


def whole(features, weight, bias, grad_out, values, rows, cols, count):
    vmem = pl.BlockSpec(memory_space=pltpu.VMEM)
    dma = pltpu.SemaphoreType.DMA
    return pl.pallas_call(
        whole_kernel,
        out_shape=(
            jax.ShapeDtypeStruct((NODE, HID), BF16),
            jax.ShapeDtypeStruct((PIECES, PIECE, HID), F32),
            jax.ShapeDtypeStruct((EXTRA, HID), F32),
            jax.ShapeDtypeStruct((NODE, WIDTH), BF16),
        ),
        in_specs=[vmem] * 4 + [pl.BlockSpec(memory_space=pl.ANY)] + [vmem] * 3,
        out_specs=(vmem,) * 4,
        scratch_shapes=[
            pltpu.VMEM((SLOTS, TILE, TILE), BF16),
            pltpu.VMEM((ROWS, NODE, WIDTH), BF16),
            pltpu.VMEM((SLOTS, TILE, WIDTH), BF16),
            pltpu.VMEM((X, YH, CORE, NODE, WIDTH), BF16),
            pltpu.VMEM((YH, X, NODE, WIDTH), BF16),
            pltpu.VMEM((YH, X, NODE, WIDTH), BF16),
            pltpu.VMEM((YH, X, NODE, WIDTH), BF16),
            pltpu.VMEM((NODE, WIDTH), BF16),
            pltpu.VMEM((NODE, WIDTH), BF16),
            pltpu.VMEM((COLS, NODE, WIDTH), BF16),
            pltpu.VMEM((Z, YL, NODE, WIDTH), BF16),
            pltpu.VMEM((2, 4, YL, NODE, WIDTH), BF16),
            pltpu.VMEM((2, 4, YL, NODE, WIDTH), BF16),
            pltpu.VMEM((YL, NODE, WIDTH), BF16),
            pltpu.VMEM((YL, NODE, WIDTH), BF16),
            pltpu.VMEM((CORE, WIDTH // CORE + EXTRA, HID), F32),
            pltpu.VMEM((WIDTH // CORE + EXTRA, HID), F32),
            pltpu.VMEM((X, WIDTH // CORE // X + EXTRA, HID), F32),
            pltpu.VMEM((X, WIDTH // CORE // X + EXTRA, HID), F32),
            pltpu.VMEM((YH, PIECE + EXTRA, HID), F32),
            pltpu.VMEM((PIECE + EXTRA, HID), F32),
            pltpu.VMEM((PIECE + EXTRA, HID), F32),
            pltpu.VMEM((YL, PIECE + EXTRA, HID), F32),
            pltpu.VMEM((PIECE + EXTRA, HID), F32),
            pltpu.VMEM((Z, PIECE + EXTRA, HID), F32),
            pltpu.VMEM((8, SLOTS), jnp.int32),
            pltpu.VMEM((8, SLOTS), F32),
            pltpu.SMEM((8, SLOTS), jnp.int32),
            pltpu.SMEM((8, SLOTS), F32),
            dma((SENDS,)),
            dma,
            dma((2,)),
            dma((ROWS,)),
            dma((ROWS,)),
            dma((YH, X)),
            dma((YH, X)),
            dma((1,)),
            dma((COLS,)),
            dma((2, 4, YL)),
            dma((YL,)),
            dma((1,)),
            dma((X,)),
            dma((1,)),
            dma((YL,)),
            dma((Z,)),
            dma((PIECES,)),
        ],
        compiler_params=pltpu.CompilerParams(
            collective_id=0, has_side_effects=True, vmem_limit_bytes=VMEM_LIMIT
        ),
    )(features, weight, bias, grad_out, values, rows, cols, count)


def finish_kernel(hidden, gw, gb, result, hidden_out, gw_out, gb_out, result_out):
    hidden_out[...] = hidden[...]
    gw_out[...] = gw[...]
    gb_out[...] = gb[0:1]
    result_out[...] = result[...]


def finish(hidden, gw, gb, result):
    vmem = pl.BlockSpec(memory_space=pltpu.VMEM)
    return pl.pallas_call(
        finish_kernel,
        out_shape=(
            jax.ShapeDtypeStruct((NODE, HID), BF16),
            jax.ShapeDtypeStruct((WIDTH, HID), F32),
            jax.ShapeDtypeStruct((1, HID), F32),
            jax.ShapeDtypeStruct((NODE, WIDTH), BF16),
        ),
        in_specs=[vmem] * 4,
        out_specs=(vmem,) * 4,
    )(hidden, gw, gb, result)


def split_rows(outs):
    hidden, gw, gb, result = outs
    return hidden, gw.reshape(WIDTH, HID), gb, result


def per_device(features, weight, bias, grad_out, tile_values, tile_rows, tile_cols, tile_count):
    hidden, grad_weight, grad_bias, grad_features = finish(*split_rows(whole(
        features, weight, bias.reshape(1, HID), grad_out, tile_values[0, 0], tile_rows[0], tile_cols[0], tile_count
    )))
    return hidden, grad_weight, grad_bias[0], grad_features


def solution(mesh):
    return jax.shard_map(
        per_device,
        mesh=mesh,
        in_specs=(
            P(("col", "row"), None),
            P(),
            P(),
            P(("row", "col"), None),
            P("row", "col", None, None, None),
            P("row", "col", None),
            P("row", "col", None),
            P("row", "col"),
        ),
        out_specs=(P(("row", "col"), None), P(), P(), P(("col", "row"), None)),
        check_vma=False,
    )
```

time: 796 us -> 105 us (0.13)
  the two profiles are of different devices: /device:TPU:6 before, /device:TPU:1 now
where the time goes in v2:
time: 105 us
  Pallas kernels  103 us (98%)
  between operations  1.29 us (1%)
    pallas_call x1, Pallas kernels, whole(): pl.pallas_call(whole_kernel, out_shape=(jax.ShapeDtypeStruct((NODE, HID),...  102 us

profile of v2, /device:TPU:1, one launch (start us, length us, event | category | flops | bytes accessed | tf_op | source)
XLA Modules:
  0.0 104.7 jit_solution(17119869971013471092)
XLA Ops:
  1.3 101.7 %shard_map.111 = (bf16[256,256]{1,0:T(8,128)(2,1)}, f32[16,8,256]{2,1,0:T(8,128)}, f32[8,256]{1,0:T(8,128)}, bf16[256,128]{1,0:T(8,128)(2,1)}) custom-call(bf16[256,128]{1,0:T(8,128)(2,1)} %feat.1, bf16[128,256]{1,0:T(8,128)(2,1)} %weight.1, f32[1,256]{1,0:T(1,128)} %bitcast.8, bf16[256,256]{1,0:T(8,128)(2,1)} %grad_out.1, bf16[128,128,128]{2,1,0:T(8,128)(2,1)} %bitcast.6, ...), custom_call_target="tpu_custom_call" | custom-call | tf_op jit(solution)/shard_map/pallas_call | solution.py:416
  103.0 1.7 %shard_map.112 = (bf16[256,256]{1,0:T(8,128)(2,1)}, f32[128,256]{1,0:T(8,128)}, f32[1,256]{1,0:T(1,128)}, bf16[256,128]{1,0:T(8,128)(2,1)}) custom-call(bf16[256,256]{1,0:T(8,128)(2,1)} %get-tuple-element.12.hidden, f32[128,256]{1,0:T(8,128)} %bitcast.7, f32[8,256]{1,0:T(8,128)} %get-tuple-element.14.gb, bf16[256,128]{1,0:T(8,128)(2,1)} %get-tuple-element.15.result), custom_call_target="tpu_custom_call" | custom-call | tf_op jit(solution)/shard_map/pallas_call | solution.py:489

commit v3 on v2

--- a/solution.py
+++ b/solution.py
@@ -20,7 +20,7 @@
 SLOTS = 128
 ROW_TILES = COLS * NODE // TILE
 COL_TILES = ROWS * NODE // TILE
-SPLIT = 192
+SPLIT = 144
 REST = NODE - SPLIT
 VMEM_LIMIT = 56 * 1024 * 1024
 
@@ -50,6 +50,7 @@
     def __init__(self, sems):
         self.sems = sems
         self.started = []
+        self.waited = 0
 
     def send(self, src, dst, recv_sem, peer):
         copy = pltpu.make_async_remote_copy(
@@ -63,9 +64,10 @@
         copy.start()
         self.started.append(copy)
 
-    def finish(self):
-        for copy in self.started:
+    def finish(self, upto=None):
+        for copy in self.started[self.waited:upto]:
             copy.wait_send()
+        self.waited = len(self.started) if upto is None else upto
 
 
 def arrived(dst, recv_sem, peer):
@@ -78,7 +80,7 @@
 PIECES = 16
 PIECE = WIDTH // PIECES
 EXTRA = 8
-UNROLL = 16
+UNROLL = 32
 GATHER_SENDS = 3 + 28 + 7 + 24
 MIDDLE_SENDS = 8 + 6 + 1 + 1 + 6 + 8
 PARAM_SENDS = 1 + 3 + 1 + 3 + 7 + 1 + 6 + 8
@@ -227,17 +229,21 @@
 
     products(0, ints, floats, values, panel.reshape(COL_TILES, TILE, WIDTH), run, 1)
     tiles_per = NODE // TILE
-    for r in range(ROW_TILES):
-        c, t = r // tiles_per, r % tiles_per
-        tile = (run[ints[2, r]].astype(F32) * floats[2, r]).astype(BF16)
-        partial[c // (YH * CORE), (c // CORE) % YH, c % CORE, t * TILE:(t + 1) * TILE] = tile
-
+    gathered = len(out.started)
     order = [2, 1, 3, 0]
-    for h in range(YH):
-        hh = (1 - yh) if h == 0 else yh
-        for d in order:
-            other = (x + d) % X
-            out.send(partial.at[other, hh, 1 - core], pair_in.at[h, d], pair_sem.at[h, d], sibling)
+
+    def result_tile(base, r):
+        return (run[ints[base, r]].astype(F32) * floats[base, r]).astype(BF16)
+
+    for c in (1 - core, core):
+        for h in range(YH):
+            hh = (1 - yh) if h == 0 else yh
+            for d in order:
+                other = (x + d) % X
+                for t in range(tiles_per):
+                    partial[other, hh, c, t * TILE:(t + 1) * TILE] = result_tile(2, col_of(other, hh, c) * tiles_per + t)
+                if c is not core:
+                    out.send(partial.at[other, hh, c], pair_in.at[h, d], pair_sem.at[h, d], sibling)
     for h in range(YH):
         hh = (1 - yh) if h == 0 else yh
         for d in order:
@@ -254,6 +260,7 @@
             acc += x_in[h, d].astype(F32)
         return acc
 
+    out.finish(gathered)
     y_out[...] = summed(0).astype(BF16)
     out.send(y_out, y_in, y_sem.at[0], far)
     own = summed(1)
@@ -284,11 +291,7 @@
         core_piece[c, :half] = gw[c * half:(c + 1) * half]
         core_piece[c, half:] = gb
     out.send(core_piece.at[1 - core], core_piece_in, core_psem.at[0], sibling)
-    c = col_of(x, 1 - yh, core)
-    arrived(*g(c), far)
-    for d in order[:3]:
-        share(c, ring[d - 1])
-    share(c, sibling)
+    out.finish(len(out.started) - 6)
     arrived(core_piece_in, core_psem.at[0], sibling)
     quarter = half // X
     for q in range(X):
@@ -296,45 +299,70 @@
             x_piece[q, at:at + size] = core_piece[core, here:here + size] + core_piece_in[here:here + size]
     for d in range(1, X):
         out.send(x_piece.at[(x + d) % X], x_piece_in.at[X - d], x_psem.at[X - d], ring[d - 1])
-    for d in (1, 3, 2):
-        for h in (yh, 1 - yh):
-            c = col_of((x + d) % X, h, core)
-            arrived(*g(c), ring[d - 1])
-            share(c, sibling)
+
+    def from_ring(d, h):
+        c = col_of((x + d) % X, h, core)
+        arrived(*g(c), ring[d - 1])
+        share(c, sibling)
+
+    from_ring(1, yh)
+    from_ring(3, yh)
+    c = col_of(x, 1 - yh, core)
+    arrived(*g(c), far)
+    for d in order[:3]:
+        share(c, ring[d - 1])
+    share(c, sibling)
+    from_ring(2, yh)
     acc = x_piece[x]
     for d in range(1, X):
         arrived(x_piece_in.at[d], x_psem.at[d], ring[d - 1])
         acc = acc + x_piece_in[d]
+    z_piece[...] = acc
+    for d in range(1, Z):
+        out.send(z_piece, z_piece_in.at[Z - d], z_psem.at[Z - d], along[d - 1])
+    for d in (1, 3, 2):
+        from_ring(d, 1 - yh)
+    for d in range(X):
+        for h in range(YH):
+            arrived(*g(col_of((x + d) % X, h, 1 - core)), sibling)
+
+    products(3, ints, floats, values, block.reshape(ROW_TILES, TILE, WIDTH), run, 0)
+    gathered = len(out.started)
+
+    ways = ((0, 1, up, down), (1, -1, down, up))
+    turns = (1, 2, 3, 0)
+
+    def own_a(dz, j):
+        return back.at[(z + Z + dz) % Z, (y + j) % YL]
+
+    def build(dz, j):
+        zz, yy = (z + Z + dz) % Z, (y + j) % YL
+        for t in range(tiles_per):
+            back[zz, yy, t * TILE:(t + 1) * TILE] = result_tile(5, row_of(zz, yy) * tiles_per + t)
+
+    def begin(step, j, way, sign, target, source):
+        build(sign * (HALF_Z - step), j)
+        out.send(own_a(sign * (HALF_Z - step), j), a_in.at[way, step, j], a_sem.at[way, step, j], target)
+
+    for j in (1, 2):
+        begin(0, j, *(ways[0] if j < 2 else ways[1]))
+    for j in (3, 0):
+        begin(0, j, *(ways[0] if j < 2 else ways[1]))
+    for j in turns:
+        begin(1, j, *(ways[1] if j < 2 else ways[0]))
+    for j in turns:
+        build(HALF_Z - 1 if j < 2 else 1 - HALF_Z, j)
+    acc = z_piece[...]
+    for d in range(1, Z):
+        arrived(z_piece_in.at[d], z_psem.at[d], along[d - 1])
+        acc = acc + z_piece_in[d]
     for h in range(YH):
         far_piece[h, :PIECE] = acc[h * PIECE:(h + 1) * PIECE]
         far_piece[h, PIECE:] = acc[quarter:]
     out.send(far_piece.at[1 - yh], far_piece_in, far_psem.at[0], far)
-    for d in range(X):
-        for h in range(YH):
-            arrived(*g(col_of((x + d) % X, h, 1 - core)), sibling)
-
-    products(3, ints, floats, values, block.reshape(ROW_TILES, TILE, WIDTH), run, 0)
-    for r in range(COL_TILES):
-        s, t = r // tiles_per, r % tiles_per
-        tile = (run[ints[5, r]].astype(F32) * floats[5, r]).astype(BF16)
-        back[s // YL, s % YL, t * TILE:(t + 1) * TILE] = tile
-
-    ways = ((0, 1, up, down), (1, -1, down, up))
-    turns = (1, 2, 3, 0)
-
-    def own_a(dz, j):
-        return back.at[(z + Z + dz) % Z, (y + j) % YL]
-
-    for j in turns:
-        way, _, target, _ = ways[0] if j < 2 else ways[1]
-        out.send(own_a(HALF_Z, j), a_in.at[way, 0, j], a_sem.at[way, 0, j], target)
-    for j in turns:
-        way, sign, target, _ = ways[1] if j < 2 else ways[0]
-        out.send(own_a(sign * (HALF_Z - 1), j), a_in.at[way, 1, j], a_sem.at[way, 1, j], target)
-    arrived(far_piece_in, far_psem.at[0], far)
-    near_piece[...] = far_piece[yh] + far_piece_in[...]
-    for j in range(1, YL):
-        out.send(near_piece, near_piece_in.at[YL - j], near_psem.at[YL - j], near[j - 1])
+    for dz in (2, -2):
+        for j in turns:
+            build(dz, j)
 
     def hop(step, j, way, sign, target, source):
         arrived(a_in.at[way, step - 1, j], a_sem.at[way, step - 1, j], source)
@@ -345,20 +373,21 @@
 
     for j in turns:
         hop(1, j, *(ways[0] if j < 2 else ways[1]))
-    acc = near_piece[...]
-    for j in range(1, YL):
-        arrived(near_piece_in.at[j], near_psem.at[j], near[j - 1])
-        acc = acc + near_piece_in[j]
-    z_piece[...] = acc
-    for d in range(1, Z):
-        out.send(z_piece, z_piece_in.at[Z - d], z_psem.at[Z - d], along[d - 1])
+    for dz in (1, -1, 0):
+        for j in turns:
+            build(dz, j)
+    out.finish(gathered)
+    arrived(far_piece_in, far_psem.at[0], far)
+    near_piece[...] = far_piece[yh] + far_piece_in[...]
+    for j in range(1, YL):
+        out.send(near_piece, near_piece_in.at[YL - j], near_psem.at[YL - j], near[j - 1])
     for j in turns:
         for way in ways:
             hop(2, j, *way)
-    acc = z_piece[...]
-    for d in range(1, Z):
-        arrived(z_piece_in.at[d], z_psem.at[d], along[d - 1])
-        acc = acc + z_piece_in[d]
+    acc = near_piece[...]
+    for j in range(1, YL):
+        arrived(near_piece_in.at[j], near_psem.at[j], near[j - 1])
+        acc = acc + near_piece_in[j]
 
     def spot(x_at, h, c):
         return (c * X + x_at) * YH + h
@@ -378,6 +407,7 @@
     for j in turns:
         for way in ways:
             hop(3, j, *way)
+    out.finish(len(out.started) - 16)
     p = spot(x, 1 - yh, core)
     arrived(*last(p), far)
     for d in range(1, X):
@@ -447,8 +477,8 @@
             pltpu.VMEM((PIECE + EXTRA, HID), F32),
             pltpu.VMEM((PIECE + EXTRA, HID), F32),
             pltpu.VMEM((YL, PIECE + EXTRA, HID), F32),
-            pltpu.VMEM((PIECE + EXTRA, HID), F32),
-            pltpu.VMEM((Z, PIECE + EXTRA, HID), F32),
+            pltpu.VMEM((WIDTH // CORE // X + EXTRA, HID), F32),
+            pltpu.VMEM((Z, WIDTH // CORE // X + EXTRA, HID), F32),
             pltpu.VMEM((8, SLOTS), jnp.int32),
             pltpu.VMEM((8, SLOTS), F32),
             pltpu.SMEM((8, SLOTS), jnp.int32),

time: 105 us -> 101 us (0.962)
  Pallas kernels: 103 us -> 100 us
    pallas_call x1, Pallas kernels: 102 us -> 98.3 us  [whole(): pl.pallas_call(whole_kernel, out_shape=(jax.ShapeDtypeStruct((NODE, HID),...]
where the time goes in v3:
time: 101 us
  Pallas kernels  100 us (99%)
  between operations  1.29 us (1%)
    pallas_call x1, Pallas kernels, whole(): pl.pallas_call(whole_kernel, out_shape=(jax.ShapeDtypeStruct((NODE, HID),...  98.3 us

profile of v3, /device:TPU:1, one launch (start us, length us, event | category | flops | bytes accessed | tf_op | source)
XLA Modules:
  0.0 101.3 jit_solution(11086591288375469918)
XLA Ops:
  1.3 98.3 %shard_map.111 = (bf16[256,256]{1,0:T(8,128)(2,1)}, f32[16,8,256]{2,1,0:T(8,128)}, f32[8,256]{1,0:T(8,128)}, bf16[256,128]{1,0:T(8,128)(2,1)}) custom-call(bf16[256,128]{1,0:T(8,128)(2,1)} %feat.1, bf16[128,256]{1,0:T(8,128)(2,1)} %weight.1, f32[1,256]{1,0:T(1,128)} %bitcast.8, bf16[256,256]{1,0:T(8,128)(2,1)} %grad_out.1, bf16[128,128,128]{2,1,0:T(8,128)(2,1)} %bitcast.6, ...), custom_call_target="tpu_custom_call" | custom-call | tf_op jit(solution)/shard_map/pallas_call | solution.py:446
  99.6 1.7 %shard_map.112 = (bf16[256,256]{1,0:T(8,128)(2,1)}, f32[128,256]{1,0:T(8,128)}, f32[1,256]{1,0:T(1,128)}, bf16[256,128]{1,0:T(8,128)(2,1)}) custom-call(bf16[256,256]{1,0:T(8,128)(2,1)} %get-tuple-element.12.hidden, f32[128,256]{1,0:T(8,128)} %bitcast.7, f32[8,256]{1,0:T(8,128)} %get-tuple-element.14.gb, bf16[256,128]{1,0:T(8,128)(2,1)} %get-tuple-element.15.result), custom_call_target="tpu_custom_call" | custom-call | tf_op jit(solution)/shard_map/pallas_call | solution.py:519

commit v4 on v3

--- a/solution.py
+++ b/solution.py
@@ -43,7 +43,10 @@
     barrier = pltpu.get_barrier_semaphore()
     for peer in peers:
         pl.semaphore_signal(barrier, inc=1, device_id=peer, device_id_type=MESH)
-    pl.semaphore_wait(barrier, len(peers))
+
+
+def greeted(count):
+    pl.semaphore_wait(pltpu.get_barrier_semaphore(), count)
 
 
 class Sender:
@@ -130,18 +133,17 @@
 
 
 def whole_kernel(
-    feat, weight, bias, grad_out, values_hbm, rows_ref, cols_ref, count_ref,
+    feat, weight_hbm, bias_hbm, grad_hbm, values_hbm, rows_hbm, cols_hbm, count_ref,
     hidden, gw_out, gb_out, result,
+    weight, bias, grad_out, rows_ref, cols_ref,
     values, panel, run, partial, paired, pair_in, x_in, y_out, y_in, block, back,
     a_out, a_in, near_out, near_in,
     core_piece, core_piece_in, x_piece, x_piece_in, far_piece, far_piece_in, near_piece, near_piece_in, z_piece, z_piece_in,
     ints_v, floats_v, ints, floats,
-    sends, values_sem, table_sem, recv_a, recv_b, pair_sem, x_sem, y_sem, gather_sem, a_sem, near_sem,
+    sends, load_sem, values_sem, table_sem, recv_a, recv_b, pair_sem, x_sem, y_sem, gather_sem, a_sem, near_sem,
     core_psem, x_psem, far_psem, near_psem, z_psem, last_sem,
 ):
     row, col, z, y, x, yh, core = where_am_i()
-    load = pltpu.make_async_copy(values_hbm, values, values_sem)
-    load.start()
     up = (row_of((z + 1) % Z, y), col)
     down = (row_of((z + Z - 1) % Z, y), col)
     near = [(row_of(z, (y + j) % YL), col) for j in range(1, YL)]
@@ -149,7 +151,23 @@
     sibling = (row, col_of(x, yh, 1 - core))
     far = (row, col_of(x, 1 - yh, core))
     ring = [(row, col_of((x + d) % X, yh, core)) for d in range(1, X)]
-    greet(near + along + [sibling, far] + ring)
+    greet([far] + along + ring + near + [sibling])
+    early = [
+        pltpu.make_async_copy(rows_hbm, rows_ref, load_sem.at[0]),
+        pltpu.make_async_copy(cols_hbm, cols_ref, load_sem.at[1]),
+    ]
+    late = [
+        pltpu.make_async_copy(feat, panel.at[row], load_sem.at[2]),
+        pltpu.make_async_copy(values_hbm, values, values_sem),
+    ]
+    dense = [
+        pltpu.make_async_copy(weight_hbm, weight, load_sem.at[3]),
+        pltpu.make_async_copy(bias_hbm, bias, load_sem.at[4]),
+        pltpu.make_async_copy(grad_hbm, grad_out, load_sem.at[5]),
+    ]
+    for copy in early + late + dense:
+        copy.start()
+    greeted(len(along + near + ring) + 2)
     out = Sender(sends)
 
     part_a, part_b = pl.ds(0, SPLIT), pl.ds(SPLIT, REST)
@@ -176,8 +194,9 @@
     pass_on(mine[0], row, a, down)
     for j in range(1, YL):
         pass_on(mine[1], row, b, near[j - 1])
-    panel[row] = feat[...]
-
+
+    for copy in early:
+        copy.wait()
     live = lax.broadcasted_iota(jnp.int32, (1, SLOTS), 1) < count_ref[...]
     ints_v[...] = jnp.zeros_like(ints_v)
     floats_v[...] = jnp.zeros_like(floats_v)
@@ -220,7 +239,8 @@
         pass_on(b(s)[0], s, b, near[j - 1])
     for copy in table:
         copy.wait()
-    load.wait()
+    for copy in late:
+        copy.wait()
     for j in range(YL):
         arrived(*a(shard(HALF_Z, j)), down if j < 2 else up)
     for dz in range(Z):
@@ -267,6 +287,8 @@
     arrived(y_in, y_sem.at[0], far)
     aggregate = (own + y_in[...].astype(F32)).astype(BF16)
 
+    for copy in dense:
+        copy.wait()
     preact = jnp.dot(aggregate, weight[...], preferred_element_type=F32) + bias[...]
     sigmoid = jax.nn.sigmoid(preact)
     slope = sigmoid * (1.0 + preact * (1.0 - sigmoid))
@@ -451,9 +473,14 @@
             jax.ShapeDtypeStruct((EXTRA, HID), F32),
             jax.ShapeDtypeStruct((NODE, WIDTH), BF16),
         ),
-        in_specs=[vmem] * 4 + [pl.BlockSpec(memory_space=pl.ANY)] + [vmem] * 3,
+        in_specs=[pl.BlockSpec(memory_space=pl.ANY)] * 7 + [vmem],
         out_specs=(vmem,) * 4,
         scratch_shapes=[
+            pltpu.VMEM((WIDTH, HID), BF16),
+            pltpu.VMEM((1, HID), F32),
+            pltpu.VMEM((NODE, HID), BF16),
+            pltpu.VMEM((1, SLOTS), jnp.int32),
+            pltpu.VMEM((1, SLOTS), jnp.int32),
             pltpu.VMEM((SLOTS, TILE, TILE), BF16),
             pltpu.VMEM((ROWS, NODE, WIDTH), BF16),
             pltpu.VMEM((SLOTS, TILE, WIDTH), BF16),
@@ -484,6 +511,7 @@
             pltpu.SMEM((8, SLOTS), jnp.int32),
             pltpu.SMEM((8, SLOTS), F32),
             dma((SENDS,)),
+            dma((6,)),
             dma,
             dma((2,)),
             dma((ROWS,)),

time: 101 us -> 101 us (level)
  no operation moved by 1% of the time
where the time goes in v4:
time: 101 us
  Pallas kernels  99.4 us (98%)
  between operations  1.29 us (1%)
    pallas_call x1, Pallas kernels, whole(): pl.pallas_call(whole_kernel, out_shape=(jax.ShapeDtypeStruct((NODE, HID),...  97.7 us

profile of v4, /device:TPU:1, one launch (start us, length us, event | category | flops | bytes accessed | tf_op | source)
XLA Modules:
  0.0 100.7 jit_solution(3996251484706170577)
XLA Ops:
  1.3 97.7 %shard_map.111 = (bf16[256,256]{1,0:T(8,128)(2,1)}, f32[16,8,256]{2,1,0:T(8,128)}, f32[8,256]{1,0:T(8,128)}, bf16[256,128]{1,0:T(8,128)(2,1)}) custom-call(bf16[256,128]{1,0:T(8,128)(2,1)} %feat.1, bf16[128,256]{1,0:T(8,128)(2,1)} %weight_hbm.1, f32[1,256]{1,0:T(1,128)} %bitcast.8, bf16[256,256]{1,0:T(8,128)(2,1)} %grad_hbm.1, ...), custom_call_target="tpu_custom_call" | custom-call | tf_op jit(solution)/shard_map/pallas_call | solution.py:468
  99.0 1.7 %shard_map.112 = (bf16[256,256]{1,0:T(8,128)(2,1)}, f32[128,256]{1,0:T(8,128)}, f32[1,256]{1,0:T(1,128)}, bf16[256,128]{1,0:T(8,128)(2,1)}) custom-call(bf16[256,256]{1,0:T(8,128)(2,1)} %get-tuple-element.12.hidden, f32[128,256]{1,0:T(8,128)} %bitcast.7, f32[8,256]{1,0:T(8,128)} %get-tuple-element.14.gb, bf16[256,128]{1,0:T(8,128)(2,1)} %get-tuple-element.15.result), custom_call_target="tpu_custom_call" | custom-call | tf_op jit(solution)/shard_map/pallas_call | solution.py:547

commit v5 on v4

--- a/solution.py
+++ b/solution.py
@@ -421,7 +421,7 @@
         out.send(gw_out.at[p], gw_out.at[p], last_sem.at[p], peer)
 
     gw_out[spot(x, yh, core)] = acc[:PIECE]
-    gb_out[...] = acc[PIECE:]
+    gb_out[...] = acc[PIECE:PIECE + 1]
     spread(spot(x, yh, core), far)
     for d in range(1, X):
         spread(spot(x, yh, core), ring[d - 1])
@@ -470,7 +470,7 @@
         out_shape=(
             jax.ShapeDtypeStruct((NODE, HID), BF16),
             jax.ShapeDtypeStruct((PIECES, PIECE, HID), F32),
-            jax.ShapeDtypeStruct((EXTRA, HID), F32),
+            jax.ShapeDtypeStruct((1, HID), F32),
             jax.ShapeDtypeStruct((NODE, WIDTH), BF16),
         ),
         in_specs=[pl.BlockSpec(memory_space=pl.ANY)] * 7 + [vmem],
@@ -535,26 +535,24 @@
     )(features, weight, bias, grad_out, values, rows, cols, count)
 
 
-def finish_kernel(hidden, gw, gb, result, hidden_out, gw_out, gb_out, result_out):
-    hidden_out[...] = hidden[...]
-    gw_out[...] = gw[...]
-    gb_out[...] = gb[0:1]
-    result_out[...] = result[...]
-
-
-def finish(hidden, gw, gb, result):
-    vmem = pl.BlockSpec(memory_space=pltpu.VMEM)
+def finish_kernel(*refs):
+    half = len(refs) // 2
+    copies = [pltpu.make_async_copy(refs[i], refs[half + i], refs[-1].at[i]) for i in range(half)]
+    for copy in copies:
+        copy.start()
+    for copy in copies:
+        copy.wait()
+
+
+def finish(*arrays):
+    anywhere = pl.BlockSpec(memory_space=pl.ANY)
     return pl.pallas_call(
         finish_kernel,
-        out_shape=(
-            jax.ShapeDtypeStruct((NODE, HID), BF16),
-            jax.ShapeDtypeStruct((WIDTH, HID), F32),
-            jax.ShapeDtypeStruct((1, HID), F32),
-            jax.ShapeDtypeStruct((NODE, WIDTH), BF16),
-        ),
-        in_specs=[vmem] * 4,
-        out_specs=(vmem,) * 4,
-    )(hidden, gw, gb, result)
+        out_shape=tuple(jax.ShapeDtypeStruct(a.shape, a.dtype) for a in arrays),
+        in_specs=[anywhere] * len(arrays),
+        out_specs=(anywhere,) * len(arrays),
+        scratch_shapes=[pltpu.SemaphoreType.DMA((len(arrays),))],
+    )(*arrays)
 
 
 def split_rows(outs):

time: 101 us -> 110 us (1.089)
  Pallas kernels: 99.4 us -> 109 us
    pallas_call x1, Pallas kernels: 1.71 us -> 11.1 us  [finish(): pl.pallas_call(finish_kernel, out_shape=tuple((jax.ShapeDtypeStruct(a.sha...]
where the time goes in v5:
time: 110 us
  Pallas kernels  109 us (99%)
  between operations  1.29 us (1%)
    pallas_call x1, Pallas kernels, whole(): pl.pallas_call(whole_kernel, out_shape=(jax.ShapeDtypeStruct((NODE, HID),...  97.7 us
    pallas_call x1, Pallas kernels, finish(): pl.pallas_call(finish_kernel, out_shape=tuple((jax.ShapeDtypeStruct(a.sha...  11.1 us

profile of v5, /device:TPU:1, one launch (start us, length us, event | category | flops | bytes accessed | tf_op | source)
XLA Modules:
  0.0 110.1 jit_solution(3983247712203096885)
XLA Ops:
  1.3 97.7 %shard_map.111 = (bf16[256,256]{1,0:T(8,128)(2,1)}, f32[16,8,256]{2,1,0:T(8,128)}, f32[1,256]{1,0:T(1,128)}, bf16[256,128]{1,0:T(8,128)(2,1)}) custom-call(bf16[256,128]{1,0:T(8,128)(2,1)} %feat.1, bf16[128,256]{1,0:T(8,128)(2,1)} %weight_hbm.1, f32[1,256]{1,0:T(1,128)} %bitcast.8, bf16[256,256]{1,0:T(8,128)(2,1)} %grad_hbm.1, ...), custom_call_target="tpu_custom_call" | custom-call | tf_op jit(solution)/shard_map/pallas_call | solution.py:468
  99.0 11.1 %shard_map.112 = (bf16[256,256]{1,0:T(8,128)(2,1)}, f32[128,256]{1,0:T(8,128)}, f32[1,256]{1,0:T(1,128)}, bf16[256,128]{1,0:T(8,128)(2,1)}) custom-call(bf16[256,256]{1,0:T(8,128)(2,1)} %get-tuple-element.12.refs_0_, f32[128,256]{1,0:T(8,128)} %bitcast.7, f32[1,256]{1,0:T(1,128)} %get-tuple-element.14.refs_2_, bf16[256,128]{1,0:T(8,128)(2,1)} %get-tuple-element.15.refs_3_), custom_call_target="tpu_custom_call" | custom-call | tf_op jit(solution)/shard_map/pallas_call | solution.py:549
